TPU v7x, 128 devices: a whole 4x4x4 slice. The times are simulated.
128 devices in a mesh: section: 2 (over core), dp: 32 (over z, y, x_hi), tensor: 2 (over x_lo).
Axes of the slice: x: 4 (x_hi: 2, x_lo: 2; x = x_hi * 2 + x_lo), y: 4, z: 4, core: 2. Of those that a mesh axis runs over, the one named last changes fastest.
Arguments:
- tokens: bfloat16 [32, 8, 48, 5120], P('dp', None, 'tensor'), may hold values from -6 to 6
- doc_ids: int32 [32, 384], P('dp'), may hold values from 0 to 3, never falling along the last dimension, each value on 1 to 192 neighbouring positions
- norm_gain: float32 [2, 5120], P('section'), may hold values from 0.1 to 1.9
- w_query: bfloat16 [2, 5120, 2560], P('section', 'dp', 'tensor'), may hold values from -0.078125 to 0.078125
- w_key: bfloat16 [2, 5120, 512], P('section', None, 'tensor'), may hold values from -0.078125 to 0.078125
- w_value: bfloat16 [2, 5120, 512], P('section', None, 'tensor'), may hold values from -0.078125 to 0.078125
- w_out: bfloat16 [2, 2560, 5120], P('section', 'tensor', 'dp'), may hold values from -0.125 to 0.125
Outputs:
- layer_states: bfloat16 [2, 32, 8, 48, 5120], P('section', 'dp', None, 'tensor')
Inputs may be any that keep to these rules, and one draw needn't show every extreme that they name: `doc_ids`: each sequence's positions are cut into consecutive whole documents numbered from 0 in order, none longer than 192 positions, one exactly that long.
All inputs are finite; a program needn't handle non-finite values.
Results may differ from a plain program's by a relative error of at most 0.018.
Values may be sent and summed in bfloat16 or wider, within the bound.
A program may use at most 128 MiB of HBM per device.

v0:
```python
import jax
import jax.numpy as jnp
from jax import lax
from jax.sharding import PartitionSpec as P

HEAD = 128


def shifted(value, axis, by):
    count = lax.axis_size(axis)
    pairs = [(i, i + by) for i in range(count) if 0 <= i + by < count]
    return lax.ppermute(value, axis, pairs)


def on_device(tokens, doc_ids, norm_gain, w_query, w_key, w_value, w_out):
    query_full = lax.all_gather(w_query[0], "dp", axis=0, tiled=True)
    out_full = lax.all_gather(w_out[0], "dp", axis=1, tiled=True)
    key_proj = w_key[0]
    value_proj = w_value[0]
    gain = norm_gain[0]
    docs = doc_ids[0]
    n_segments = tokens.shape[1]
    quarter = tokens.shape[2]
    width = tokens.shape[3]
    seg_rows = quarter * lax.axis_size("tensor")
    seq_rows = n_segments * seg_rows
    section = lax.axis_index("section")
    ticks = n_segments + lax.axis_size("section") - 1
    kv_width = key_proj.shape[1]
    kv_local = kv_width // HEAD
    q_width = query_full.shape[1]
    group = q_width // HEAD // kv_local
    scale = 1.0 / HEAD**0.5

    def attend(rows_full, slot, key_cache, value_cache):
        wide = rows_full.astype(jnp.float32)
        normed = (
            wide * lax.rsqrt(jnp.mean(wide * wide, axis=-1, keepdims=True) + 1e-06) * gain
        ).astype(jnp.bfloat16)
        query = jnp.dot(normed, query_full, preferred_element_type=jnp.float32).astype(jnp.bfloat16)
        key = jnp.dot(normed, key_proj, preferred_element_type=jnp.float32).astype(jnp.bfloat16)
        value = jnp.dot(normed, value_proj, preferred_element_type=jnp.float32).astype(jnp.bfloat16)
        first = slot * seg_rows
        key_cache = lax.dynamic_update_slice_in_dim(key_cache, key, first, 0)
        value_cache = lax.dynamic_update_slice_in_dim(value_cache, value, first, 0)
        grouped = query.reshape(seg_rows, kv_local, group, HEAD)
        keys = key_cache.reshape(seq_rows, kv_local, HEAD)
        values = value_cache.reshape(seq_rows, kv_local, HEAD)
        scores = (
            jnp.einsum("qkgd,skd->kgqs", grouped, keys, preferred_element_type=jnp.float32) * scale
        )
        query_pos = first + jnp.arange(seg_rows, dtype=jnp.int32)
        key_pos = jnp.arange(seq_rows, dtype=jnp.int32)
        query_docs = lax.dynamic_slice_in_dim(docs, first, seg_rows, 0)
        allowed = (key_pos[None, :] <= query_pos[:, None]) & (docs[None, :] == query_docs[:, None])
        scores = jnp.where(allowed[None, None], scores, -1e30)
        weights = jax.nn.softmax(scores, axis=-1).astype(jnp.bfloat16)
        attended = jnp.einsum("kgqs,skd->qkgd", weights, values, preferred_element_type=jnp.float32)
        return (attended.astype(jnp.bfloat16).reshape(seg_rows, q_width), key_cache, value_cache)

    def resting(rows_full, slot, key_cache, value_cache):
        return (jnp.zeros((seg_rows, q_width), jnp.bfloat16), key_cache, value_cache)

    def project(attended, active):

        def doing(block):
            return jnp.dot(block, out_full, preferred_element_type=jnp.float32)

        def skipping(block):
            return jnp.zeros((block.shape[0], width), jnp.float32)

        return lax.cond(active, doing, skipping, attended)

    empty_cache = jnp.zeros((seq_rows, kv_width), jnp.bfloat16)
    empty_stash = jnp.zeros((n_segments, quarter, width), jnp.bfloat16)

    def tick(step, carry):
        incoming, key_cache, value_cache, stash = carry
        slot_raw = step - section
        active = jnp.logical_and(slot_raw >= 0, slot_raw < n_segments)
        slot = jnp.clip(slot_raw, 0, n_segments - 1)
        own = jnp.where(section == 0, lax.dynamic_index_in_dim(tokens[0], slot, 0, False), incoming)
        rows_full = lax.all_gather(own, "tensor", axis=0, tiled=True)
        attended, key_cache, value_cache = lax.cond(
            active, attend, resting, rows_full, slot, key_cache, value_cache
        )
        summed = lax.psum_scatter(
            project(attended, active).astype(jnp.bfloat16),
            "tensor",
            scatter_dimension=0,
            tiled=True,
        ).astype(jnp.float32)
        new_rows = (own.astype(jnp.float32) + summed).astype(jnp.bfloat16)
        stash = jnp.where(active, lax.dynamic_update_index_in_dim(stash, new_rows, slot, 0), stash)
        passed = shifted(new_rows, "section", 1)
        return (passed, key_cache, value_cache, stash)

    start_rows = jnp.zeros((quarter, width), jnp.bfloat16)
    final = lax.fori_loop(0, ticks, tick, (start_rows, empty_cache, empty_cache, empty_stash))
    return final[3][None, None]


def solution(mesh):
    in_specs = (
        P("dp", None, "tensor", None),
        P("dp", None),
        P("section", None),
        P("section", "dp", "tensor"),
        P("section", None, "tensor"),
        P("section", None, "tensor"),
        P("section", "tensor", "dp"),
    )
    out_specs = P("section", "dp", None, "tensor", None)
    return jax.shard_map(
        on_device, mesh=mesh, in_specs=in_specs, out_specs=out_specs, check_vma=False
    )
```

profile of v0, /device:TPU:1, one launch (start us, length us, event | category | flops | bytes accessed | tf_op | source)
XLA Modules:
  0.0 911.4 jit_solution(3911308124100008832)
XLA Ops:
  9.3 137.5 %all-gather.7.cloned.1.call-done = bf16[1,1280,5120]{1,2,0:T(8,128)(2,1)} async-done(((bf16[1,1280,160]{1,2,0:T(8,128)(2,1)}), bf16[1,1280,5120]{1,2,0:T(8,128)(2,1)}) %all-gather.7.cloned.1.call-update) | async-done | bytes 13107216 | tf_op jit(solution)/shard_map/all_gather | solution.py:17
  146.8 17.9 %copy.21 = bf16[1280,5120]{1,0:T(8,128)(2,1)} copy(bf16[1280,5120]{0,1:T(8,128)(2,1)} %bitcast.39) | data formatting | bytes 26214400 | tf_op jit(solution)/shard_map/while | solution.py:99
  164.7 116.7 %all-gather.5.cloned.1.call-done = bf16[1,5120,1280]{2,1,0:T(8,128)(2,1)} async-done(((bf16[1,160,1280]{2,1,0:T(8,128)(2,1)}), bf16[1,5120,1280]{2,1,0:T(8,128)(2,1)}) %all-gather.5.cloned.1.call-update) | async-done | bytes 13107216 | tf_op jit(solution)/shard_map/all_gather | solution.py:16
  283.7 621.2 %while.20 = (s32[]{:T(128)}, bf16[24,5120]{1,0:T(8,128)(2,1)S(1)}, bf16[384,256]{1,0:T(8,128)(2,1)}, bf16[384,256]{1,0:T(8,128)(2,1)S(1)}, bf16[8,24,5120]{2,1,0...) while((s32[]{:T(128)}, bf16[24,5120]{1,0:T(8,128)(2,1)S(1)}, ...), condition=%wide.region_9.10_spmd, body=%wide.region_0.9_spmd.sunk | while | flops 1657793920 | bytes 47733248 | solution.py:99
  293.3 51.6 %reduce-scatter.2.cloned.1.call-done = bf16[24,5120]{1,0:T(8,128)(2,1)} async-done(((bf16[48,5120]{1,0:T(8,128)(2,1)}), bf16[24,5120]{1,0:T(8,128)(2,1)}) %reduce-scatter.2.cloned.1.call-update) | async-done | bytes 245776 | tf_op jit(solution)/shard_map/while/body/eval_jaxpr/reduce_scatter | solution.py:87
  351.2 8.1 all_gather.17
  359.3 29.0 %conditional.4 = (bf16[48,1280]{1,0:T(8,128)(2,1)}, bf16[384,256]{1,0:T(8,128)(2,1)}, bf16[384,256]{1,0:T(8,128)(2,1)S(1)}) conditional(s32[]{:T(128)} %convert_element_type.99, (bf16[384,256]{1,0:T(8,128)(2,1)}, bf16[384,256]{1,0:T(8,128)(2,1)S(1)}) %tuple.55, (bf16[48,5120]{1,0:T(8,128)(2,1)S(1)}, f32[1,5120]{1,0:T(1,128)}, ...), branch_computations={%region_1.1_spmd, %region_2.5_spmd} | conditional | flops 1027911040 | bytes 26146350 | solution.py:84
  368.4 7.8 convolution_convert_fusion
  388.3 7.2 conditional.5
  396.3 18.1 %reduce-scatter.2.cloned.1.call-done = bf16[24,5120]{1,0:T(8,128)(2,1)} async-done(((bf16[48,5120]{1,0:T(8,128)(2,1)}), bf16[24,5120]{1,0:T(8,128)(2,1)}) %reduce-scatter.2.cloned.1.call-update) | async-done | bytes 245776 | tf_op jit(solution)/shard_map/while/body/eval_jaxpr/reduce_scatter | solution.py:87
  420.6 8.1 all_gather.17
  428.7 29.0 %conditional.4 = (bf16[48,1280]{1,0:T(8,128)(2,1)}, bf16[384,256]{1,0:T(8,128)(2,1)}, bf16[384,256]{1,0:T(8,128)(2,1)S(1)}) conditional(s32[]{:T(128)} %convert_element_type.99, (bf16[384,256]{1,0:T(8,128)(2,1)}, bf16[384,256]{1,0:T(8,128)(2,1)S(1)}) %tuple.55, (bf16[48,5120]{1,0:T(8,128)(2,1)S(1)}, f32[1,5120]{1,0:T(1,128)}, ...), branch_computations={%region_1.1_spmd, %region_2.5_spmd} | conditional | flops 1027911040 | bytes 26146350 | solution.py:84
  437.8 7.8 convolution_convert_fusion
  457.7 7.2 conditional.5
  457.7 7.2 fusion.31
  465.7 18.1 %reduce-scatter.2.cloned.1.call-done = bf16[24,5120]{1,0:T(8,128)(2,1)} async-done(((bf16[48,5120]{1,0:T(8,128)(2,1)}), bf16[24,5120]{1,0:T(8,128)(2,1)}) %reduce-scatter.2.cloned.1.call-update) | async-done | bytes 245776 | tf_op jit(solution)/shard_map/while/body/eval_jaxpr/reduce_scatter | solution.py:87
  490.0 8.1 all_gather.17
  498.1 29.0 %conditional.4 = (bf16[48,1280]{1,0:T(8,128)(2,1)}, bf16[384,256]{1,0:T(8,128)(2,1)}, bf16[384,256]{1,0:T(8,128)(2,1)S(1)}) conditional(s32[]{:T(128)} %convert_element_type.99, (bf16[384,256]{1,0:T(8,128)(2,1)}, bf16[384,256]{1,0:T(8,128)(2,1)S(1)}) %tuple.55, (bf16[48,5120]{1,0:T(8,128)(2,1)S(1)}, f32[1,5120]{1,0:T(1,128)}, ...), branch_computations={%region_1.1_spmd, %region_2.5_spmd} | conditional | flops 1027911040 | bytes 26146350 | solution.py:84
  507.2 7.8 convolution_convert_fusion
  527.1 7.2 conditional.5
  527.1 7.2 fusion.31
  535.1 18.1 %reduce-scatter.2.cloned.1.call-done = bf16[24,5120]{1,0:T(8,128)(2,1)} async-done(((bf16[48,5120]{1,0:T(8,128)(2,1)}), bf16[24,5120]{1,0:T(8,128)(2,1)}) %reduce-scatter.2.cloned.1.call-update) | async-done | bytes 245776 | tf_op jit(solution)/shard_map/while/body/eval_jaxpr/reduce_scatter | solution.py:87
  559.4 8.1 all_gather.17
  567.5 29.0 %conditional.4 = (bf16[48,1280]{1,0:T(8,128)(2,1)}, bf16[384,256]{1,0:T(8,128)(2,1)}, bf16[384,256]{1,0:T(8,128)(2,1)S(1)}) conditional(s32[]{:T(128)} %convert_element_type.99, (bf16[384,256]{1,0:T(8,128)(2,1)}, bf16[384,256]{1,0:T(8,128)(2,1)S(1)}) %tuple.55, (bf16[48,5120]{1,0:T(8,128)(2,1)S(1)}, f32[1,5120]{1,0:T(1,128)}, ...), branch_computations={%region_1.1_spmd, %region_2.5_spmd} | conditional | flops 1027911040 | bytes 26146350 | solution.py:84
  576.6 7.8 convolution_convert_fusion
  596.5 7.2 conditional.5
  604.5 18.2 %reduce-scatter.2.cloned.1.call-done = bf16[24,5120]{1,0:T(8,128)(2,1)} async-done(((bf16[48,5120]{1,0:T(8,128)(2,1)}), bf16[24,5120]{1,0:T(8,128)(2,1)}) %reduce-scatter.2.cloned.1.call-update) | async-done | bytes 245776 | tf_op jit(solution)/shard_map/while/body/eval_jaxpr/reduce_scatter | solution.py:87
  628.9 8.1 all_gather.17
  637.0 29.0 %conditional.4 = (bf16[48,1280]{1,0:T(8,128)(2,1)}, bf16[384,256]{1,0:T(8,128)(2,1)}, bf16[384,256]{1,0:T(8,128)(2,1)S(1)}) conditional(s32[]{:T(128)} %convert_element_type.99, (bf16[384,256]{1,0:T(8,128)(2,1)}, bf16[384,256]{1,0:T(8,128)(2,1)S(1)}) %tuple.55, (bf16[48,5120]{1,0:T(8,128)(2,1)S(1)}, f32[1,5120]{1,0:T(1,128)}, ...), branch_computations={%region_1.1_spmd, %region_2.5_spmd} | conditional | flops 1027911040 | bytes 26146350 | solution.py:84
  646.1 7.8 convolution_convert_fusion
  666.0 7.2 conditional.5
  674.0 18.1 %reduce-scatter.2.cloned.1.call-done = bf16[24,5120]{1,0:T(8,128)(2,1)} async-done(((bf16[48,5120]{1,0:T(8,128)(2,1)}), bf16[24,5120]{1,0:T(8,128)(2,1)}) %reduce-scatter.2.cloned.1.call-update) | async-done | bytes 245776 | tf_op jit(solution)/shard_map/while/body/eval_jaxpr/reduce_scatter | solution.py:87
  698.3 8.1 all_gather.17
  706.4 29.0 %conditional.4 = (bf16[48,1280]{1,0:T(8,128)(2,1)}, bf16[384,256]{1,0:T(8,128)(2,1)}, bf16[384,256]{1,0:T(8,128)(2,1)S(1)}) conditional(s32[]{:T(128)} %convert_element_type.99, (bf16[384,256]{1,0:T(8,128)(2,1)}, bf16[384,256]{1,0:T(8,128)(2,1)S(1)}) %tuple.55, (bf16[48,5120]{1,0:T(8,128)(2,1)S(1)}, f32[1,5120]{1,0:T(1,128)}, ...), branch_computations={%region_1.1_spmd, %region_2.5_spmd} | conditional | flops 1027911040 | bytes 26146350 | solution.py:84
  715.6 7.8 convolution_convert_fusion
  735.4 7.2 conditional.5
  743.4 18.1 %reduce-scatter.2.cloned.1.call-done = bf16[24,5120]{1,0:T(8,128)(2,1)} async-done(((bf16[48,5120]{1,0:T(8,128)(2,1)}), bf16[24,5120]{1,0:T(8,128)(2,1)}) %reduce-scatter.2.cloned.1.call-update) | async-done | bytes 245776 | tf_op jit(solution)/shard_map/while/body/eval_jaxpr/reduce_scatter | solution.py:87
  767.7 8.1 all_gather.17
  775.8 29.0 %conditional.4 = (bf16[48,1280]{1,0:T(8,128)(2,1)}, bf16[384,256]{1,0:T(8,128)(2,1)}, bf16[384,256]{1,0:T(8,128)(2,1)S(1)}) conditional(s32[]{:T(128)} %convert_element_type.99, (bf16[384,256]{1,0:T(8,128)(2,1)}, bf16[384,256]{1,0:T(8,128)(2,1)S(1)}) %tuple.55, (bf16[48,5120]{1,0:T(8,128)(2,1)S(1)}, f32[1,5120]{1,0:T(1,128)}, ...), branch_computations={%region_1.1_spmd, %region_2.5_spmd} | conditional | flops 1027911040 | bytes 26146350 | solution.py:84
  785.0 7.8 convolution_convert_fusion
  804.8 7.2 conditional.5
  804.8 7.2 fusion.31
  812.8 18.1 %reduce-scatter.2.cloned.1.call-done = bf16[24,5120]{1,0:T(8,128)(2,1)} async-done(((bf16[48,5120]{1,0:T(8,128)(2,1)}), bf16[24,5120]{1,0:T(8,128)(2,1)}) %reduce-scatter.2.cloned.1.call-update) | async-done | bytes 245776 | tf_op jit(solution)/shard_map/while/body/eval_jaxpr/reduce_scatter | solution.py:87
  837.2 8.1 all_gather.17
  845.3 29.0 %conditional.4 = (bf16[48,1280]{1,0:T(8,128)(2,1)}, bf16[384,256]{1,0:T(8,128)(2,1)}, bf16[384,256]{1,0:T(8,128)(2,1)S(1)}) conditional(s32[]{:T(128)} %convert_element_type.99, (bf16[384,256]{1,0:T(8,128)(2,1)}, bf16[384,256]{1,0:T(8,128)(2,1)S(1)}) %tuple.55, (bf16[48,5120]{1,0:T(8,128)(2,1)S(1)}, f32[1,5120]{1,0:T(1,128)}, ...), branch_computations={%region_1.1_spmd, %region_2.5_spmd} | conditional | flops 1027911040 | bytes 26146350 | solution.py:84
  854.4 7.8 convolution_convert_fusion
  874.3 7.2 conditional.5
  882.3 17.3 %reduce-scatter.2.cloned.1.call-done = bf16[24,5120]{1,0:T(8,128)(2,1)} async-done(((bf16[48,5120]{1,0:T(8,128)(2,1)}), bf16[24,5120]{1,0:T(8,128)(2,1)}) %reduce-scatter.2.cloned.1.call-update) | async-done | bytes 245776 | tf_op jit(solution)/shard_map/while/body/eval_jaxpr/reduce_scatter | solution.py:87
  (269 shorter events, 281.3 us)
Async XLA Ops:
  6.5 140.3 %all-gather.7.cloned.1.call-start = ((), (), s32[]{:S(2)}) async-start(), calls=%async_computation.2 | async-start | bytes 13516800 | tf_op jit(solution)/shard_map/all_gather | solution.py:17
  7.3 274.2 %all-gather.5.cloned.1.call-start = ((), (), s32[]{:S(2)}) async-start(), calls=%async_computation.1 | async-start | bytes 13516800 | tf_op jit(solution)/shard_map/all_gather | solution.py:16
  146.8 136.8 %copy-start = (bf16[1,5120,256]{2,1,0:T(8,128)(2,1)S(1)}, bf16[1,5120,256]{2,1,0:T(8,128)(2,1)}, u32[]{:S(2)}) copy-start(bf16[1,5120,256]{2,1,0:T(8,128)(2,1)} %param.18) | copy-start | bytes 7864324
  283.7 61.2 %reduce-scatter.2.cloned.1.call-start = ((), (), s32[]{:S(2)}) async-start(), calls=%async_computation.3 | async-start | bytes 737280 | tf_op jit(solution)/shard_map/while/body/eval_jaxpr/reduce_scatter | solution.py:87
  292.5 0.8 copy-start.1
  346.8 3.4 collective-permute-start
  350.2 64.2 %reduce-scatter.2.cloned.1.call-start = ((), (), s32[]{:S(2)}) async-start(), calls=%async_computation.3 | async-start | bytes 737280 | tf_op jit(solution)/shard_map/while/body/eval_jaxpr/reduce_scatter | solution.py:87
  359.3 0.7 copy-start.2
  359.5 0.5 copy-start.4
  384.0 4.2 copy-start.3
  395.5 0.8 copy-start.1
  416.2 3.4 collective-permute-start
  419.6 64.2 %reduce-scatter.2.cloned.1.call-start = ((), (), s32[]{:S(2)}) async-start(), calls=%async_computation.3 | async-start | bytes 737280 | tf_op jit(solution)/shard_map/while/body/eval_jaxpr/reduce_scatter | solution.py:87
  428.7 0.7 copy-start.2
  453.4 4.2 copy-start.3
  464.8 0.8 copy-start.1
  485.6 3.4 collective-permute-start
  489.0 64.2 %reduce-scatter.2.cloned.1.call-start = ((), (), s32[]{:S(2)}) async-start(), calls=%async_computation.3 | async-start | bytes 737280 | tf_op jit(solution)/shard_map/while/body/eval_jaxpr/reduce_scatter | solution.py:87
  498.1 0.7 copy-start.2
  522.9 4.2 copy-start.3
  534.3 0.8 copy-start.1
  555.1 3.4 collective-permute-start
  558.4 64.2 %reduce-scatter.2.cloned.1.call-start = ((), (), s32[]{:S(2)}) async-start(), calls=%async_computation.3 | async-start | bytes 737280 | tf_op jit(solution)/shard_map/while/body/eval_jaxpr/reduce_scatter | solution.py:87
  567.5 0.7 copy-start.2
  592.3 4.2 copy-start.3
  603.7 0.8 copy-start.1
  624.5 3.4 collective-permute-start
  627.9 64.2 %reduce-scatter.2.cloned.1.call-start = ((), (), s32[]{:S(2)}) async-start(), calls=%async_computation.3 | async-start | bytes 737280 | tf_op jit(solution)/shard_map/while/body/eval_jaxpr/reduce_scatter | solution.py:87
  637.0 0.7 copy-start.2
  637.2 0.5 copy-start.4
  661.8 4.2 copy-start.3
  673.2 0.8 copy-start.1
  694.0 3.4 collective-permute-start
  697.3 64.2 %reduce-scatter.2.cloned.1.call-start = ((), (), s32[]{:S(2)}) async-start(), calls=%async_computation.3 | async-start | bytes 737280 | tf_op jit(solution)/shard_map/while/body/eval_jaxpr/reduce_scatter | solution.py:87
  706.4 0.7 copy-start.2
  731.2 4.2 copy-start.3
  742.6 0.8 copy-start.1
  763.4 3.4 collective-permute-start
  766.8 64.2 %reduce-scatter.2.cloned.1.call-start = ((), (), s32[]{:S(2)}) async-start(), calls=%async_computation.3 | async-start | bytes 737280 | tf_op jit(solution)/shard_map/while/body/eval_jaxpr/reduce_scatter | solution.py:87
  775.8 0.7 copy-start.2
  800.6 4.2 copy-start.3
  812.0 0.8 copy-start.1
  832.8 3.4 collective-permute-start
  836.2 63.4 %reduce-scatter.2.cloned.1.call-start = ((), (), s32[]{:S(2)}) async-start(), calls=%async_computation.3 | async-start | bytes 737280 | tf_op jit(solution)/shard_map/while/body/eval_jaxpr/reduce_scatter | solution.py:87
  845.3 0.7 copy-start.2
  870.0 4.2 copy-start.3
  881.5 0.8 copy-start.1
  901.4 3.4 collective-permute-start
  (6 other events, 3.3 us)
Sparse Core Ops, SparseCore 0:
  10.5 136.2 all-gather.6
  150.0 131.4 all-gather.4
  293.4 51.4 reduce-scatter.1
  396.4 17.9 reduce-scatter.1
  465.8 17.9 reduce-scatter.1
  535.2 17.9 reduce-scatter.1
  604.6 17.9 reduce-scatter.1
  674.1 17.9 reduce-scatter.1
  743.5 17.9 reduce-scatter.1
  812.9 17.9 reduce-scatter.1
  882.4 17.1 reduce-scatter.1
where the time goes:
time: 915 us; the launch traced here: 911 us
  waiting for transfers between devices  470 us (51%)
  matrix products  211 us (23%)
  local copies, waits for them, and re-layouts  79.2 us (9%)
  blocking collectives  71.8 us (8%)
  other arithmetic  53.6 us (6%)
  between operations  13.1 us (1%)
  starting transfers between devices  11.6 us (1%)
    reduce_scatter x9, waiting for transfers between devices, tick(): lax.psum_scatter(project(attended, active).astype(jnp.bfloat16), 'tensor'...  196 us
    all_gather x1, waiting for transfers between devices, on_device(): out_full = lax.all_gather(w_out[0], 'dp', axis=1, tiled=True)  138 us
    all_gather x1, waiting for transfers between devices, on_device(): query_full = lax.all_gather(w_query[0], 'dp', axis=0, tiled=True)  117 us
    all_gather x9, blocking collectives, tick(): rows_full = lax.all_gather(own, 'tensor', axis=0, tiled=True)  71.8 us
    dot_general x8, matrix products, attend(): jnp.dot(normed, query_full, preferred_element_type=jnp.float32)  62.7 us
    dot_general x8, matrix products, doing(): return jnp.dot(block, out_full, preferred_element_type=jnp.float32)  57.5 us
    dot_general x8, matrix products, attend(): jnp.dot(normed, key_proj, preferred_element_type=jnp.float32)  23.7 us
    ppermute x9, waiting for transfers between devices, shifted(): return lax.ppermute(value, axis, pairs)  18.9 us
  transfers between devices with their start and end apart: 20, of which 20 were waited for; matrix products, arithmetic and copies ran while one was open for 2% of the time, Pallas kernels for 0%

commit v1 on v0

v1 whole, which is shorter than its diff:
```python
import functools

import jax
import jax.numpy as jnp
from jax import lax
from jax.experimental import pallas as pl
from jax.experimental.pallas import tpu as pltpu
from jax.sharding import PartitionSpec as P

HEAD = 128
MESH = pl.DeviceIdType.MESH
RING = 4
PARTS = 8
ORDER = (0, 3, 1, 2)


def layer_kernel(
    tok, docs_col, docs_row, pos_col, pos_row, gain, wq, wot, wk, wv, out,
    full_q, full_o, kv_w, hidden, normed, query, key, value, attended, bias, part, part_in, fresh,
    w_recv, w_send, x_recv, x_send, own_sem, kv_sem, h_sem, h_send, p_recv, p_send, n_send, o_sem, gate,
):
    section = lax.axis_index("section")
    dp = lax.axis_index("dp")
    tensor = lax.axis_index("tensor")
    z, y, far = dp // 8, (dp // 2) % RING, dp % 2
    rows = tok.shape[0]
    seq = 2 * rows
    width = tok.shape[1]
    block = wq.shape[0]
    half = block // 2
    q_width = wq.shape[1]
    chunk = width // PARTS
    weights = (full_q, full_o)
    shards = (wq, wot)

    def at(dz, dy):
        return (section, ((z + dz) % RING) * 8 + ((y + dy) % RING) * 2 + far, tensor)

    opposite = (section, z * 8 + y * 2 + (1 - far), tensor)
    partner = (section, dp, 1 - tensor)
    core = (1 - section, dp, tensor)
    partner_core = (1 - section, dp, 1 - tensor)
    peers = [at(1, 0), at(-1, 0), at(0, 1), at(0, -1), opposite, partner, core, partner_core]
    barrier = pltpu.get_barrier_semaphore()
    for peer in peers:
        pl.semaphore_signal(barrier, inc=1, device_id=peer, device_id_type=MESH)

    def zy(cls, fo, go):
        return (fo, go) if cls == 0 else (go, fo)

    def piece(w, cls, fo, go, h):
        dz, dy = zy(cls, fo, go)
        first = (((z + dz) % RING) * 8 + ((y + dy) % RING) * 2 + cls) * block + h * half
        return weights[w].at[pl.ds(pl.multiple_of(first, 16), half), :]

    def own_piece(w, which, h):
        first = (z * 8 + y * 2 + which) * block + h * half
        return weights[w].at[pl.ds(pl.multiple_of(first, 16), half), :]

    def send_of(w, cls, fo, go, h, along_f, step):
        src = piece(w, cls, fo, go, h)
        to_fo = (fo - step) % RING if along_f else fo
        to_go = go if along_f else (go - step) % RING
        dz, dy = zy(cls, step, 0) if along_f else zy(cls, 0, step)
        return pltpu.make_async_remote_copy(
            src_ref=src,
            dst_ref=src,
            send_sem=w_send.at[w, cls, to_fo * 4 + to_go, h],
            recv_sem=w_recv.at[w, cls, to_fo * 4 + to_go, h],
            device_id=at(dz, dy),
            device_id_type=MESH,
        )

    def wait_piece(w, cls, fo, go, h):
        ref = piece(w, cls, fo, go, h)
        pltpu.make_async_remote_copy(
            src_ref=ref, dst_ref=ref, send_sem=w_send.at[w, cls, fo * 4 + go, h],
            recv_sem=w_recv.at[w, cls, fo * 4 + go, h], device_id=at(1, 0), device_id_type=MESH,
        ).wait_recv()

    sends = []

    def send(*which):
        copy = send_of(*which)
        copy.start()
        sends.append(which)

    def across(w, h):
        return pltpu.make_async_remote_copy(
            src_ref=shards[w].at[pl.ds(h * half, half), :], dst_ref=own_piece(w, far, h),
            send_sem=x_send.at[w, h], recv_sem=x_recv.at[w, h], device_id=opposite, device_id_type=MESH,
        )

    def across_in(w, h):
        ref = own_piece(w, 1 - far, h)
        pltpu.make_async_remote_copy(
            src_ref=ref, dst_ref=ref, send_sem=x_send.at[w, h], recv_sem=x_recv.at[w, h],
            device_id=opposite, device_id_type=MESH,
        ).wait_recv()

    def own_copy(w, h):
        return pltpu.make_async_copy(
            shards[w].at[pl.ds(h * half, half), :], own_piece(w, far, h), own_sem.at[w, h]
        )

    def first_sends(w, cls, log):
        for h in (0, 1):
            for along_f in (True, False):
                for step in ((1, -1) if h == 0 else (-1, 1)):
                    which = (w, cls, 0, 0, h, along_f, step)
                    send_of(*which).start()
                    if log:
                        sends.append(which)

    def open_gather(w):
        for cls in (0, 1):
            for h in (0, 1):
                for along_f in (True, False):
                    for step in (1, -1):
                        sends.append((w, cls, 0, 0, h, along_f, step))
        for mine in (0, 1):

            @pl.when(far == mine)
            def _():
                for h in (0, 1):
                    own_copy(w, h).wait()
                first_sends(w, mine, False)
                for h in (0, 1):
                    across_in(w, h)
                first_sends(w, 1 - mine, False)

    def spread(w, cls, fo, h):
        def event():
            wait_piece(w, cls, fo, 0, h)
            if fo == 3 and h == 0:
                send(w, cls, fo, 0, h, True, 1)
            if fo == 1 and h == 1:
                send(w, cls, fo, 0, h, True, -1)
            send(w, cls, fo, 0, h, False, 1)
            send(w, cls, fo, 0, h, False, -1)

        return event

    def relay(w, cls, fo, go):
        def event():
            h = 0 if go == 3 else 1
            wait_piece(w, cls, fo, go, h)
            send(w, cls, fo, go, h, False, 1 if go == 3 else -1)

        return event

    def events_of(w):
        early, late = [], []
        for fo, h in ((3, 0), (1, 1), (3, 1), (1, 0), (2, 0), (2, 1)):
            for cls in (0, 1):
                early.append(spread(w, cls, fo, h))
        for fo in ORDER:
            for cls in (0, 1):
                for go in (3, 1):
                    late.append(relay(w, cls, fo, go))
        return early, late

    def rest_of(w, cls, fo, go):
        for h in (0, 1):
            if not (go == 3 and h == 0) and not (go == 1 and h == 1):
                wait_piece(w, cls, fo, go, h)

    def rows_of(which):
        return pl.ds(pl.multiple_of(which * rows, 16), rows)

    def cols_of(k):
        first = ((z + ORDER[k // 2]) % RING) * (2 * chunk) + (k % 2) * chunk
        return pl.ds(pl.multiple_of(first, 128), chunk)

    kv_copies = [
        pltpu.make_async_copy(wk, kv_w.at[0], kv_sem.at[0]),
        pltpu.make_async_copy(wv, kv_w.at[1], kv_sem.at[1]),
    ]
    for h in (0, 1):
        own_copy(0, h).start()
    for h in (0, 1):
        own_copy(1, h).start()
    for copy in kv_copies:
        copy.start()
    pl.semaphore_wait(barrier, len(peers))
    for w in (0, 1):
        for h in (0, 1):
            across(w, h).start()

    def token_copy(k):
        return pltpu.make_async_copy(
            tok.at[:, cols_of(k)], hidden.at[rows_of(tensor), cols_of(k)], h_sem.at[0, k]
        )

    def token_send(k):
        return pltpu.make_async_remote_copy(
            src_ref=tok.at[:, cols_of(k)], dst_ref=hidden.at[rows_of(tensor), cols_of(k)],
            send_sem=h_send.at[k], recv_sem=h_sem.at[1, k], device_id=partner, device_id_type=MESH,
        )

    @pl.when(section == 0)
    def _():
        for k in range(PARTS):
            token_copy(k).start()
            token_send(k).start()

    @pl.when(section == 1)
    def _():
        pl.semaphore_wait(gate, 1)

    early_q, late_q = events_of(0)
    early_o, late_o = events_of(1)
    open_gather(0)
    for event in early_q:
        event()
    for event in late_q[:12]:
        event()
    open_gather(1)
    for event in late_q[12:]:
        event()

    allowed = (pos_row[...] <= pos_col[...]) & (docs_row[...] == docs_col[...])
    bias[...] = jnp.where(allowed, 0.0, -1e30)

    pending = early_o + late_o[:12]

    def pump(count):
        for _ in range(min(count, len(pending))):
            pending.pop(0)()

    pump(4)
    for k in range(PARTS):
        for src, whose in ((0, tensor), (1, 1 - tensor)):
            ref = hidden.at[rows_of(whose), cols_of(k)]
            pltpu.make_async_copy(ref, ref, h_sem.at[src, k]).wait()
    pump(2)

    step_rows = 16

    def normalise(i, _):
        place = pl.ds(pl.multiple_of(i * step_rows, step_rows), step_rows)
        wide = hidden[place, :].astype(jnp.float32)
        level = lax.rsqrt(jnp.mean(wide * wide, axis=-1, keepdims=True) + 1e-06)
        normed[place, :] = (wide * level * gain[...]).astype(jnp.bfloat16)
        return 0

    lax.fori_loop(0, seq // step_rows, normalise, 0)
    pump(3)
    for copy in kv_copies:
        copy.wait()
    key[...] = jnp.dot(normed[...], kv_w[0], preferred_element_type=jnp.float32).astype(jnp.bfloat16)
    value[...] = jnp.dot(normed[...], kv_w[1], preferred_element_type=jnp.float32).astype(jnp.bfloat16)
    pump(3)

    for cls in (0, 1):
        for fo in range(RING):
            for go in (3, 1, 2):
                rest_of(0, cls, fo, go)

    tile = 256

    def project(i, _):
        cols = pl.ds(pl.multiple_of(i * tile, tile), tile)
        query[:, cols] = jnp.dot(
            normed[...], full_q[:, cols], preferred_element_type=jnp.float32
        ).astype(jnp.bfloat16)
        return 0

    tiles = q_width // tile
    lax.fori_loop(0, 2, project, 0)
    pump(3)
    lax.fori_loop(2, tiles, project, 0)
    pump(3)

    scale = 1.0 / HEAD**0.5
    heads = q_width // HEAD
    group = heads // (key.shape[1] // HEAD)

    def attend(kv, h):
        cols = pl.ds(pl.multiple_of(h * HEAD, HEAD), HEAD)
        kv_cols = pl.ds(kv * HEAD, HEAD)
        scores = lax.dot_general(
            query[:, cols], key[:, kv_cols], (((1,), (1,)), ((), ())), preferred_element_type=jnp.float32
        )
        scores = scores * scale + bias[...]
        scores = jnp.exp(scores - jnp.max(scores, axis=-1, keepdims=True))
        mix = (scores / jnp.sum(scores, axis=-1, keepdims=True)).astype(jnp.bfloat16)
        attended[:, cols] = jnp.dot(
            mix, value[:, kv_cols], preferred_element_type=jnp.float32
        ).astype(jnp.bfloat16)

    for kv in range(heads // group):
        for lo, hi in ((0, 3), (3, group)):
            lax.fori_loop(kv * group + lo, kv * group + hi, lambda h, c, kv=kv: (attend(kv, h), c)[1], 0)
            pump(2)
    pump(len(pending))

    @pl.when(section == 0)
    def _():
        pl.semaphore_signal(gate, inc=1, device_id=core, device_id_type=MESH)

    def part_send(k):
        return pltpu.make_async_remote_copy(
            src_ref=part.at[k, rows_of(1 - tensor), :], dst_ref=part_in.at[k],
            send_sem=p_send.at[k], recv_sem=p_recv.at[k], device_id=partner, device_id_type=MESH,
        )

    def out_copy(k):
        return pltpu.make_async_copy(fresh.at[:, cols_of(k)], out.at[:, cols_of(k)], o_sem.at[k])

    def next_send(k, side):
        return pltpu.make_async_remote_copy(
            src_ref=fresh.at[:, cols_of(k)], dst_ref=hidden.at[rows_of(tensor), cols_of(k)],
            send_sem=n_send.at[side, k], recv_sem=h_sem.at[side, k],
            device_id=core if side == 0 else partner_core, device_id_type=MESH,
        )

    def finish(k):
        part_send(k).wait_recv()
        own = hidden[rows_of(tensor), cols_of(k)].astype(jnp.float32)
        update = part[k, rows_of(tensor), :].astype(jnp.float32) + part_in[k].astype(jnp.float32)
        fresh[:, cols_of(k)] = (own + update).astype(jnp.bfloat16)
        out_copy(k).start()

        @pl.when(section == 0)
        def _():
            next_send(k, 0).start()
            next_send(k, 1).start()

    for k in range(PARTS):
        if k % 2 == 0:
            slab = ORDER[k // 2]
            if slab == 3:
                for event in late_o[12:]:
                    event()
            if slab == 0:
                for fo in range(RING):
                    if fo:
                        pass
                for go in (3, 1, 2):
                    rest_of(1, 0, 0, go)
            else:
                for go in (3, 1, 2):
                    rest_of(1, 0, slab, go)
                for fo in range(RING):
                    rest_of(1, 1, fo, slab)
        result = lax.dot_general(
            attended[...], full_o[cols_of(k), :], (((1,), (1,)), ((), ())), preferred_element_type=jnp.float32
        )
        part[k] = result.astype(jnp.bfloat16)
        part_send(k).start()
        if k >= 2:
            finish(k - 2)
    finish(PARTS - 2)
    finish(PARTS - 1)

    for which in sends:
        send_of(*which).wait_send()
    for w in (0, 1):
        for h in (0, 1):
            across(w, h).wait_send()
    for k in range(PARTS):
        part_send(k).wait_send()
        out_copy(k).wait()

    @pl.when(section == 0)
    def _():
        for k in range(PARTS):
            token_send(k).wait_send()
            next_send(k, 0).wait_send()
            next_send(k, 1).wait_send()


def on_device(tokens, doc_ids, norm_gain, w_query, w_key, w_value, w_out):
    n_segments, quarter, width = tokens.shape[1:]
    rows = n_segments * quarter
    seq = 2 * rows
    block, q_width = w_query.shape[1:]
    kv_width = w_key.shape[2]
    chunk = width // PARTS
    docs = doc_ids[0].reshape(n_segments, 2, quarter).transpose(1, 0, 2).reshape(seq)
    pos = jnp.arange(seq, dtype=jnp.int32).reshape(n_segments, 2, quarter).transpose(1, 0, 2).reshape(seq)
    bf16 = jnp.bfloat16
    dma = pltpu.SemaphoreType.DMA
    anywhere = pl.BlockSpec(memory_space=pl.ANY)
    vmem = pl.BlockSpec(memory_space=pltpu.VMEM)
    state = pl.pallas_call(
        layer_kernel,
        out_shape=jax.ShapeDtypeStruct((rows, width), bf16),
        in_specs=[anywhere] + [vmem] * 5 + [anywhere] * 4,
        out_specs=anywhere,
        scratch_shapes=[
            pltpu.VMEM((width, q_width), bf16),
            pltpu.VMEM((width, q_width), bf16),
            pltpu.VMEM((2, width, kv_width), bf16),
            pltpu.VMEM((seq, width), bf16),
            pltpu.VMEM((seq, width), bf16),
            pltpu.VMEM((seq, q_width), bf16),
            pltpu.VMEM((seq, kv_width), bf16),
            pltpu.VMEM((seq, kv_width), bf16),
            pltpu.VMEM((seq, q_width), bf16),
            pltpu.VMEM((seq, seq), jnp.float32),
            pltpu.VMEM((PARTS, seq, chunk), bf16),
            pltpu.VMEM((PARTS, rows, chunk), bf16),
            pltpu.VMEM((rows, width), bf16),
            dma((2, 2, RING * RING, 2)),
            dma((2, 2, RING * RING, 2)),
            dma((2, 2)),
            dma((2, 2)),
            dma((2, 2)),
            dma((2,)),
            dma((2, PARTS)),
            dma((PARTS,)),
            dma((PARTS,)),
            dma((PARTS,)),
            dma((2, PARTS)),
            dma((PARTS,)),
            pltpu.SemaphoreType.REGULAR,
        ],
        compiler_params=pltpu.CompilerParams(
            collective_id=0, has_side_effects=True, vmem_limit_bytes=60 * 1024 * 1024
        ),
        name="layers",
    )(
        tokens[0].reshape(rows, width),
        docs.reshape(seq, 1),
        docs.reshape(1, seq),
        pos.reshape(seq, 1),
        pos.reshape(1, seq),
        norm_gain,
        w_query[0],
        w_out[0].T,
        w_key[0],
        w_value[0],
    )
    return state.reshape(1, 1, n_segments, quarter, width)


def solution(mesh):
    in_specs = (
        P("dp", None, "tensor", None),
        P("dp", None),
        P("section", None),
        P("section", "dp", "tensor"),
        P("section", None, "tensor"),
        P("section", None, "tensor"),
        P("section", "tensor", "dp"),
    )
    out_specs = P("section", "dp", None, "tensor", None)
    return jax.shard_map(
        on_device, mesh=mesh, in_specs=in_specs, out_specs=out_specs, check_vma=False
    )
```

time: 915 us -> 179 us (0.20)
  waiting for transfers between devices: 470 us -> 0 us
  matrix products: 211 us -> 0 us
  Pallas kernels: 0 us -> 172 us
  local copies, waits for them, and re-layouts: 79.2 us -> 5.94 us
  blocking collectives: 71.8 us -> 0 us
  other arithmetic: 53.6 us -> 0.7 us
  between operations: 13.1 us -> 0.03 us
  starting transfers between devices: 11.6 us -> 0 us
    all_gather x2 -> x0, waiting for transfers between devices: 254 us -> none  [the longest x1 138 us: on_device(): out_full = lax.all_gather(w_out[0], 'dp', axis=1, tiled=True)]
    reduce_scatter x9 -> x0, waiting for transfers between devices: 196 us -> none  [tick(): lax.psum_scatter(project(attended, active).astype(jnp.bfloat16), 'tensor'...]
    dot_general x48 -> x0, matrix products: 195 us -> none  [the longest x8 62.7 us: attend(): jnp.dot(normed, query_full, preferred_element_type=jnp.float32)]
    pallas_call x0 -> x1, Pallas kernels: none -> 172 us  [on_device(): pl.pallas_call(layer_kernel, out_shape=jax.ShapeDtypeStruct((rows, width)...]
    all_gather x9 -> x0, blocking collectives: 71.8 us -> none  [tick(): rows_full = lax.all_gather(own, 'tensor', axis=0, tiled=True)]
    reshape x32 -> x2, local copies, waits for them, and re-layouts: 36.5 us -> 1.45 us  [on_device(): jnp.arange(seq, dtype=jnp.int32).reshape(n_segments, 2, quarter)]
    select_n x18 -> x0, other arithmetic: 25.4 us -> none  [the longest x9 16.7 us: tick(): jnp.where(active, lax.dynamic_update_index_in_dim(stash, new_rows, slot,...]
    while x19 -> x0, local copies, waits for them, and re-layouts: 24.8 us -> none  [the longest x1 17.9 us: on_device(): lax.fori_loop(0, ticks, tick, (start_rows, empty_cache, empty_cache, empt...]
  transfers between devices with their start and end apart: 20 -> 0, of which waited for: 20 -> 0; matrix products, arithmetic and copies ran while one was open for 2% -> 0% of each run, Pallas kernels for 0% -> 0%
where the time goes in v1:
time: 179 us
  Pallas kernels  172 us (96%)
  local copies, waits for them, and re-layouts  5.94 us (3%)
    pallas_call x1, Pallas kernels, on_device(): pl.pallas_call(layer_kernel, out_shape=jax.ShapeDtypeStruct((rows, width)...  172 us

profile of v1, /device:TPU:1, one launch (start us, length us, event | category | flops | bytes accessed | tf_op | source)
XLA Modules:
  0.0 178.7 jit_solution(8614049842307243599)
XLA Ops:
  0.0 0.7 reduce
  0.7 0.1 reshape_squeeze.7
  0.8 0.7 reshape_reshape.9.docs_row
  1.5 0.7 reshape.125.pos_row
  2.1 0.8 reshape.127.pos_col
  2.9 0.8 reshape_reshape.10.docs_col
  3.7 172.0 %layers.1 = bf16[192,5120]{1,0:T(8,128)(2,1)} custom-call(bf16[192,5120]{1,0:T(8,128)(2,1)} %bitcast.14, s32[384,1]{1,0:T(8,128)} %reshape_reshape.10.docs_col, s32[1,384]{1,0:T(1,128)} %reshape_reshape.9.docs_row, s32[384,1]{1,0:T(8,128)} %reshape.127.pos_col, s32[1,384]{1,0:T(1,128)} %reshape.125.pos_row, f32[1,5120]{1,0:T(1,128)} %gain.1, ...), custom_call_target="tpu_custom_call" | custom-call | tf_op jit(solution)/shard_map/layers/pallas_call | solution.py:387
  175.7 2.9 %copy.15 = bf16[1,1,8,24,5120]{4,3,2,1,0:T(8,128)(2,1)} copy(bf16[1,1,8,24,5120]{4,3,2,1,0:T(8,128)(2,1)} %bitcast.11) | data formatting | bytes 3932160
  (2 shorter events, 0.0 us)

commit v2 on v1

v2 whole, which is shorter than its diff:
```python
import jax
import jax.numpy as jnp
from jax import lax
from jax.experimental import pallas as pl
from jax.experimental.pallas import tpu as pltpu
from jax.sharding import PartitionSpec as P

HEAD = 128
MESH = pl.DeviceIdType.MESH
RING = 4
PARTS = 8
ORDER = (0, 1, 3, 2)

START, SPREAD, CROSS, RELAY, LAST = range(5)
CROSS_LAST = (((0, 3), (0, 3)), ((3, 1), (0,)))
Q_EVENTS = (
    (1, 0, 3), (1, 0, 1), (2, 0, 0), (1, 1, 3), (1, 1, 1), (3, 1, 0, 0, 3), (3, 1, 0, 0, 1), (2, 1, 0),
    (3, 0, 0, 0, 3), (3, 0, 0, 0, 1), (1, 0, 2), (2, 0, 3), (3, 0, 3, 0, 3), (3, 0, 3, 0, 1), (3, 1, 3, 0, 1),
    (3, 1, 3, 0, 3), (2, 0, 1), (3, 0, 1, 0, 3), (3, 0, 1, 0, 1), (3, 1, 1, 0, 1), (3, 1, 1, 0, 3), (2, 1, 3),
    (4, 1, 0), (1, 1, 2), (2, 1, 1), (4, 0, 0), (4, 1, 3), (3, 0, 2, 0, 1), (2, 0, 2), (3, 0, 2, 0, 3),
    (3, 1, 2, 0, 1), (4, 0, 3), (2, 1, 2), (3, 0, 1, 1, 1), (3, 1, 2, 0, 3), (3, 1, 1, 1, 1), (3, 0, 1, 1, 3),
    (3, 1, 1, 1, 3), (3, 1, 2, 1, 1), (3, 0, 2, 1, 1), (3, 1, 2, 1, 3), (3, 0, 2, 1, 3),
)
O_EVENTS = (
    (2, 0, 0), (1, 0, 1), (1, 1, 1), (1, 0, 3), (1, 1, 3), (2, 1, 0), (3, 1, 0, 0, 1), (3, 0, 0, 0, 1),
    (3, 1, 0, 0, 3), (3, 0, 0, 0, 3), (2, 0, 1), (3, 0, 0, 1, 1), (3, 1, 1, 0, 1), (3, 1, 1, 0, 3), (3, 0, 0, 1, 3),
    (2, 1, 1), (1, 0, 2), (3, 0, 1, 0, 1), (3, 1, 3, 0, 1), (3, 0, 1, 0, 3), (2, 0, 3), (3, 1, 3, 0, 3),
    (3, 0, 3, 0, 1), (3, 0, 3, 0, 3), (2, 1, 3), (1, 1, 2), (4, 1, 0), (2, 0, 2), (3, 1, 1, 1, 1), (2, 1, 2),
    (3, 1, 1, 1, 3), (3, 0, 2, 0, 1), (3, 1, 3, 1, 1), (3, 0, 2, 0, 3), (3, 1, 2, 0, 1), (4, 0, 1), (3, 1, 3, 1, 3),
    (3, 1, 2, 0, 3), (3, 1, 2, 1, 1), (3, 0, 2, 1, 1), (4, 0, 3), (3, 1, 2, 1, 3), (3, 0, 2, 1, 3),
)


def needs_and_sends(w, event):
    if event[0] == START:
        sends = []
        for cls in (0, 1):
            own = (w, cls, 0, 0, 0, None)
            sends += [(own, 0, 1), (own, 0, -1), (own, 2, 0)]
        for cls in (0, 1):
            own = (w, cls, 0, 0, 0, None)
            sends += [(own, 1, 1), (own, 1, -1)]
        return [], sends
    cls, fo = event[1:3]
    if event[0] == SPREAD:
        whole = (w, cls, 0, fo, 0, None)
        needs = [whole] if fo != 2 else [whole[:5] + (0,), whole[:5] + (1,)]
        sends = []
        if fo == 3:
            sends.append((whole[:5] + (0,), 0, 1))
        if fo == 1:
            sends.append((whole[:5] + (1,), 0, -1))
        return needs, sends + [(whole, 2, 0), (whole, 1, 1), (whole, 1, -1)]
    if event[0] == CROSS:
        whole = (w, cls, 1, fo, 0, None)
        return [whole], [(whole, 1, 1), (whole, 1, -1)]
    if event[0] == RELAY:
        who, go = event[3:]
        whole = (w, cls, who, fo, go, None)
        return [whole], [(whole[:5] + (0 if go == 3 else 1,), 1, 1 if go == 3 else -1)]
    whole = (w, cls, 0, fo, 2, None)
    return [whole[:5] + (0,), whole[:5] + (1,)], [(whole, 2, 0)]


def landing(piece, link, step):
    w, cls, who, fo, go, h = piece
    if link == 0:
        return (w, cls, who, (fo - step) % RING, go, h)
    if link == 1:
        return (w, cls, who, fo, (go - step) % RING, h)
    return (w, cls, 1 - who, fo, go, h)


def in_slab(piece, offset):
    return (piece[3] if piece[1] == 0 else piece[4]) == offset


def layer_kernel(
    tok, docs_col, docs_row, pos_col, pos_row, gain, wq, wot, wk, wv, out,
    full_q, full_o, kv_w, hidden, scaled, level, acc_q, acc_kv, query, kv_made, kv, attended, bias, part, part_in, fresh,
    w_recv, w_send, own_sem, swap_send, kvw_sem, kv_sem, kv_send, h_sem, h_send, p_recv, p_send, n_send, o_sem, gate,
):
    section = lax.axis_index("section")
    dp = lax.axis_index("dp")
    tensor = lax.axis_index("tensor")
    z, y, far = dp // 8, (dp // 2) % RING, dp % 2
    rows, width = tok.shape
    seq = 2 * rows
    block, q_width = wq.shape
    half = block // 2
    small = half // 32 * 16
    chunk = width // PARTS
    slab = 2 * chunk
    kv_width = wk.shape[1]
    weights = (full_q, full_o)
    shards = (wq, wot)

    def at(dz, dy):
        return (section, ((z + dz) % RING) * 8 + ((y + dy) % RING) * 2 + far, tensor)

    opposite = (section, z * 8 + y * 2 + (1 - far), 1 - tensor)
    partner = (section, dp, 1 - tensor)
    core = (1 - section, dp, tensor)
    partner_core = (1 - section, dp, 1 - tensor)
    peers = [at(1, 0), at(-1, 0), at(0, 1), at(0, -1), opposite, partner, core, partner_core]
    barrier = pltpu.get_barrier_semaphore()
    for peer in peers:
        pl.semaphore_signal(barrier, inc=1, device_id=peer, device_id_type=MESH)

    def place(piece):
        w, cls, who, fo, go, h = piece
        dz, dy = (fo, go) if cls == 0 else (go, fo)
        whose = far if who == 0 else 1 - far
        first = (((z + dz) % RING) * 8 + ((y + dy) % RING) * 2 + whose) * block + cls * half
        large = half - small
        cut = large if who == 0 else small
        size = half
        if h == 0:
            size = cut
        if h == 1:
            first, size = first + cut, half - cut
        return weights[w].at[pl.ds(pl.multiple_of(first, 16), size), :]

    def number(piece):
        w, cls, who, fo, go, h = piece
        return w, cls, who, fo * RING + go, 1 if h == 1 else 0

    def copy_of(piece, link, step):
        name = landing(piece, link, step)
        if link == 2:
            target = opposite
        else:
            target = at(step, 0) if link == piece[1] else at(0, step)
        return pltpu.make_async_remote_copy(
            src_ref=place(piece), dst_ref=place(piece), send_sem=w_send.at[number(name)],
            recv_sem=w_recv.at[number(name)], device_id=target, device_id_type=MESH,
        )

    def await_piece(piece):
        ref = place(piece)
        pltpu.make_async_copy(ref, ref, w_recv.at[number(piece)]).wait()

    def own_copy(w, cls):
        return pltpu.make_async_copy(
            shards[w].at[pl.ds(cls * half, half), :], place((w, cls, 0, 0, 0, None)), own_sem.at[w, cls]
        )

    def swap_copy(w, cls):
        return pltpu.make_async_remote_copy(
            src_ref=shards[w].at[pl.ds(cls * half, half), :], dst_ref=place((w, cls, 0, 0, 0, None)),
            send_sem=swap_send.at[w, cls], recv_sem=own_sem.at[w, cls], device_id=partner, device_id_type=MESH,
        )

    def signal_core():
        @pl.when(section == 0)
        def _():
            pl.semaphore_signal(gate, inc=1, device_id=core, device_id_type=MESH)

    def run(w, event):
        needs, sends = needs_and_sends(w, event)
        if event[0] == START:
            for cls in (0, 1):
                own_copy(w, cls).wait()
        for piece in needs:
            await_piece(piece)
        for send in sends:
            copy_of(*send).start()

    events = ([(START,)] + list(Q_EVENTS), [(START,)] + list(O_EVENTS))
    all_sends = [send for w in (0, 1) for event in events[w] for send in needs_and_sends(w, event)[1]]
    awaited = {piece for w in (0, 1) for event in events[w] for piece in needs_and_sends(w, event)[0]}

    def rest_of(w, offset):
        for send in all_sends:
            name = landing(*send)
            if name[0] == w and name not in awaited and in_slab(name, offset):
                await_piece(name)

    def rows_of(which):
        return pl.ds(pl.multiple_of(which * rows, 16), rows)

    def cols_of(k):
        first = ((z + ORDER[k // 2]) % RING) * slab + (k % 2) * chunk
        return pl.ds(pl.multiple_of(first, 128), chunk)

    def slab_of(j):
        return pl.ds(pl.multiple_of(((z + ORDER[j]) % RING) * slab, 128), slab)

    kvw_copies = [
        pltpu.make_async_copy(wk, kv_w.at[0], kvw_sem.at[0]),
        pltpu.make_async_copy(wv, kv_w.at[1], kvw_sem.at[1]),
    ]

    def token_copy(k):
        return pltpu.make_async_copy(
            tok.at[:, cols_of(k)], hidden.at[rows_of(tensor), cols_of(k)], h_sem.at[0, k]
        )

    def token_send(k):
        return pltpu.make_async_remote_copy(
            src_ref=tok.at[:, cols_of(k)], dst_ref=hidden.at[rows_of(tensor), cols_of(k)],
            send_sem=h_send.at[k], recv_sem=h_sem.at[1, k], device_id=partner, device_id_type=MESH,
        )

    def swap(w):
        @pl.when(far == 1)
        def _():
            for cls in (0, 1):
                swap_copy(w, cls).start()

    @pl.when(far == 0)
    def _():
        for w in (0, 1):
            for cls in (0, 1):
                own_copy(w, cls).start()

    pl.semaphore_wait(barrier, len(peers))

    @pl.when(section == 0)
    def _():
        swap(0)
        for k in range(PARTS):
            if k == PARTS - 2:
                swap(1)
            token_copy(k).start()
            token_send(k).start()

    for copy in kvw_copies:
        copy.start()

    allowed = (pos_row[...] <= pos_col[...]) & (docs_row[...] == docs_col[...])
    bias[...] = jnp.where(allowed, 0.0, -1e30)
    for copy in kvw_copies:
        copy.wait()

    step_rows = 32

    def prepare(j):
        for k in (2 * j, 2 * j + 1):
            for src, whose in ((0, tensor), (1, 1 - tensor)):
                ref = hidden.at[rows_of(whose), cols_of(k)]
                pltpu.make_async_copy(ref, ref, h_sem.at[src, k]).wait()
        cols = slab_of(j)

        def body(i, carry):
            here = pl.ds(pl.multiple_of(i * step_rows, step_rows), step_rows)
            wide = hidden[here, cols].astype(jnp.float32)
            scaled[j, here, :] = (wide * gain[:, cols]).astype(jnp.bfloat16)
            total = jnp.sum(wide * wide, axis=-1, keepdims=True)
            level[here, :] = total if j == 0 else level[here, :] + total
            return carry

        lax.fori_loop(0, seq // step_rows, body, 0)
        for i in (0, 1):
            cols_i = pl.ds(i * kv_width, kv_width)
            term = jnp.dot(scaled[j], kv_w[i, slab_of(j), :], preferred_element_type=jnp.float32)
            acc_kv[:, cols_i] = term if j == 0 else acc_kv[:, cols_i] + term

    tile = 256

    def project(j):
        def body(i, carry):
            cols = pl.ds(pl.multiple_of(i * tile, tile), tile)
            term = jnp.dot(scaled[j], full_q[slab_of(j), cols], preferred_element_type=jnp.float32)
            acc_q[:, cols] = term if j == 0 else acc_q[:, cols] + term
            return carry

        lax.fori_loop(0, q_width // tile, body, 0)

    def kv_exchange(i):
        return pltpu.make_async_remote_copy(
            src_ref=kv_made.at[i], dst_ref=kv.at[i], send_sem=kv_send.at[i], recv_sem=kv_sem.at[i],
            device_id=partner, device_id_type=MESH,
        )

    def kv_keep(i):
        return pltpu.make_async_copy(kv_made.at[i], kv.at[i], kv_sem.at[i])

    def finish_kv():
        factor = lax.rsqrt(level[...] / width + 1e-06)
        level[...] = factor
        for i in (0, 1):
            kv_made[i] = (acc_kv[:, i * kv_width : (i + 1) * kv_width] * factor).astype(jnp.bfloat16)

            @pl.when(far == 1)
            def _():
                kv_exchange(i).start()

            @pl.when(far == 0)
            def _():
                kv_keep(i).start()

    def finish_q():
        for i in range(q_width // tile):
            query[:, i * tile : (i + 1) * tile] = (acc_q[:, i * tile : (i + 1) * tile] * level[...]).astype(jnp.bfloat16)

    early = 24

    @pl.when(section == 0)
    def _():
        q_events, o_events = list(events[0]), list(events[1])

        def pump(w, count):
            todo = (q_events, o_events)[w]
            for _ in range(min(count, len(todo))):
                run(w, todo.pop(0))

        pump(0, 1 + 20)
        prepare(0)
        pump(0, 8)
        prepare(1)
        pump(0, 6)
        prepare(2)
        pump(0, len(q_events))
        pump(1, 1)
        prepare(3)
        signal_core()
        finish_kv()
        for j in range(RING):
            rest_of(0, ORDER[j])
            project(j)
            pump(1, 4)
        finish_q()
        pump(1, early - 17)

    @pl.when(section == 1)
    def _():
        pl.semaphore_wait(gate, 1)
        for w in (0, 1):
            swap(w)
        pl.semaphore_wait(gate, 1)
        q_events, o_events = list(events[0]), list(events[1])

        def pump(w, count):
            todo = (q_events, o_events)[w]
            for _ in range(min(count, len(todo))):
                run(w, todo.pop(0))

        pump(0, 1 + 30)
        prepare(0)
        pump(0, len(q_events))
        pump(1, 1)
        prepare(1)
        pump(1, 3)
        for j in range(RING):
            if j >= 2:
                prepare(j)
            if j == 3:
                finish_kv()
            rest_of(0, ORDER[j])
            project(j)
            pump(1, 4)
        finish_q()
        pump(1, early - 20)

    todo = list(events[1])[early:]

    def pump(count):
        for _ in range(min(count, len(todo))):
            run(1, todo.pop(0))

    scale = 1.0 / HEAD**0.5
    heads = q_width // HEAD
    group = heads // (kv_width // HEAD)

    def attend(n, h):
        cols = pl.ds(pl.multiple_of(h * HEAD, HEAD), HEAD)
        kv_cols = pl.ds(n * HEAD, HEAD)
        scores = lax.dot_general(
            query[:, cols], kv[0, :, kv_cols], (((1,), (1,)), ((), ())), preferred_element_type=jnp.float32
        )
        scores = scores * scale + bias[...]
        scores = jnp.exp(scores - jnp.max(scores, axis=-1, keepdims=True))
        mix = (scores / jnp.sum(scores, axis=-1, keepdims=True)).astype(jnp.bfloat16)
        attended[:, cols] = jnp.dot(
            mix, kv[1, :, kv_cols], preferred_element_type=jnp.float32
        ).astype(jnp.bfloat16)

    for i in (0, 1):
        kv_keep(i).wait()
    for n in range(heads // group):
        for lo, hi in ((0, 3), (3, group)):
            lax.fori_loop(n * group + lo, n * group + hi, lambda h, c, n=n: (attend(n, h), c)[1], 0)
            pump(2)

    def part_send(k):
        return pltpu.make_async_remote_copy(
            src_ref=part.at[k, rows_of(1 - tensor), :], dst_ref=part_in.at[k],
            send_sem=p_send.at[k], recv_sem=p_recv.at[k], device_id=partner, device_id_type=MESH,
        )

    def out_copy(k):
        return pltpu.make_async_copy(fresh.at[:, cols_of(k)], out.at[:, cols_of(k)], o_sem.at[k])

    def next_send(k, side):
        return pltpu.make_async_remote_copy(
            src_ref=fresh.at[:, cols_of(k)], dst_ref=hidden.at[rows_of(tensor), cols_of(k)],
            send_sem=n_send.at[side, k], recv_sem=h_sem.at[side, k],
            device_id=core if side == 0 else partner_core, device_id_type=MESH,
        )

    def finish(k):
        part_send(k).wait_recv()
        own = hidden[rows_of(tensor), cols_of(k)].astype(jnp.float32)
        update = part[k, rows_of(tensor), :].astype(jnp.float32) + part_in[k].astype(jnp.float32)
        fresh[:, cols_of(k)] = (own + update).astype(jnp.bfloat16)
        out_copy(k).start()

        @pl.when(section == 0)
        def _():
            next_send(k, 0).start()
            next_send(k, 1).start()

    def waits_in(event, offset):
        return any(in_slab(piece, offset) for piece in needs_and_sends(1, event)[0])

    for k in range(PARTS):
        if k % 2 == 0:
            while any(waits_in(event, ORDER[k // 2]) for event in todo):
                pump(1)
            if k == 2:
                pump(len(todo))
                signal_core()
            rest_of(1, ORDER[k // 2])
        result = lax.dot_general(
            attended[...], full_o[cols_of(k), :], (((1,), (1,)), ((), ())), preferred_element_type=jnp.float32
        )
        part[k] = result.astype(jnp.bfloat16)
        part_send(k).start()
        if k >= 2:
            finish(k - 2)
    finish(PARTS - 2)
    finish(PARTS - 1)

    for send in all_sends:
        copy_of(*send).wait_send()
    for k in range(PARTS):
        part_send(k).wait_send()
        out_copy(k).wait()

    @pl.when(far == 1)
    def _():
        for w in (0, 1):
            for cls in (0, 1):
                swap_copy(w, cls).wait_send()
        for i in (0, 1):
            kv_exchange(i).wait_send()

    @pl.when(section == 0)
    def _():
        for k in range(PARTS):
            token_send(k).wait_send()
            next_send(k, 0).wait_send()
            next_send(k, 1).wait_send()


def on_device(tokens, doc_ids, norm_gain, w_query, w_key, w_value, w_out):
    n_segments, quarter, width = tokens.shape[1:]
    rows = n_segments * quarter
    seq = 2 * rows
    block, q_width = w_query.shape[1:]
    kv_width = w_key.shape[2]
    chunk = width // PARTS
    docs = doc_ids[0].reshape(n_segments, 2, quarter).transpose(1, 0, 2).reshape(seq)
    pos = jnp.arange(seq, dtype=jnp.int32).reshape(n_segments, 2, quarter).transpose(1, 0, 2).reshape(seq)
    bf16, f32 = jnp.bfloat16, jnp.float32
    dma = pltpu.SemaphoreType.DMA
    anywhere = pl.BlockSpec(memory_space=pl.ANY)
    vmem = pl.BlockSpec(memory_space=pltpu.VMEM)
    state = pl.pallas_call(
        layer_kernel,
        out_shape=jax.ShapeDtypeStruct((rows, width), bf16),
        in_specs=[anywhere] + [vmem] * 5 + [anywhere] * 4,
        out_specs=anywhere,
        scratch_shapes=[
            pltpu.VMEM((width, q_width), bf16),
            pltpu.VMEM((width, q_width), bf16),
            pltpu.VMEM((2, width, kv_width), bf16),
            pltpu.VMEM((seq, width), bf16),
            pltpu.VMEM((RING, seq, 2 * chunk), bf16),
            pltpu.VMEM((seq, 1), f32),
            pltpu.VMEM((seq, q_width), f32),
            pltpu.VMEM((seq, 2 * kv_width), f32),
            pltpu.VMEM((seq, q_width), bf16),
            pltpu.VMEM((2, seq, kv_width), bf16),
            pltpu.VMEM((2, seq, kv_width), bf16),
            pltpu.VMEM((seq, q_width), bf16),
            pltpu.VMEM((seq, seq), f32),
            pltpu.VMEM((PARTS, seq, chunk), bf16),
            pltpu.VMEM((PARTS, rows, chunk), bf16),
            pltpu.VMEM((rows, width), bf16),
            dma((2, 2, 2, RING * RING, 2)),
            dma((2, 2, 2, RING * RING, 2)),
            dma((2, 2)),
            dma((2, 2)),
            dma((2,)),
            dma((2,)),
            dma((2,)),
            dma((2, PARTS)),
            dma((PARTS,)),
            dma((PARTS,)),
            dma((PARTS,)),
            dma((2, PARTS)),
            dma((PARTS,)),
            pltpu.SemaphoreType.REGULAR,
        ],
        compiler_params=pltpu.CompilerParams(
            collective_id=0, has_side_effects=True, vmem_limit_bytes=60 * 1024 * 1024
        ),
        name="layers",
    )(
        tokens[0].reshape(rows, width),
        docs.reshape(seq, 1),
        docs.reshape(1, seq),
        pos.reshape(seq, 1),
        pos.reshape(1, seq),
        norm_gain,
        w_query[0],
        w_out[0].T,
        w_key[0],
        w_value[0],
    )
    return state.reshape(1, 1, n_segments, quarter, width)


def solution(mesh):
    in_specs = (
        P("dp", None, "tensor", None),
        P("dp", None),
        P("section", None),
        P("section", "dp", "tensor"),
        P("section", None, "tensor"),
        P("section", None, "tensor"),
        P("section", "tensor", "dp"),
    )
    out_specs = P("section", "dp", None, "tensor", None)
    return jax.shard_map(
        on_device, mesh=mesh, in_specs=in_specs, out_specs=out_specs, check_vma=False
    )
```

time: 179 us -> 169 us (0.944)
  Pallas kernels: 172 us -> 163 us
    pallas_call x1, Pallas kernels: 172 us -> 163 us  [on_device(): pl.pallas_call(layer_kernel, out_shape=jax.ShapeDtypeStruct((rows, width)...]
where the time goes in v2:
time: 169 us
  Pallas kernels  163 us (96%)
  local copies, waits for them, and re-layouts  5.94 us (4%)
    pallas_call x1, Pallas kernels, on_device(): pl.pallas_call(layer_kernel, out_shape=jax.ShapeDtypeStruct((rows, width)...  163 us

profile of v2, /device:TPU:1, one launch (start us, length us, event | category | flops | bytes accessed | tf_op | source)
XLA Modules:
  0.0 169.2 jit_solution(9925803026894461027)
XLA Ops:
  0.0 0.7 reduce
  0.7 0.1 reshape_squeeze.7
  0.8 0.7 reshape_reshape.9.docs_row
  1.5 0.7 reshape.125.pos_row
  2.1 0.8 reshape.127.pos_col
  2.9 0.8 reshape_reshape.10.docs_col
  3.7 162.6 %layers.1 = bf16[192,5120]{1,0:T(8,128)(2,1)} custom-call(bf16[192,5120]{1,0:T(8,128)(2,1)} %bitcast.14, s32[384,1]{1,0:T(8,128)} %reshape_reshape.10.docs_col, s32[1,384]{1,0:T(1,128)} %reshape_reshape.9.docs_row, s32[384,1]{1,0:T(8,128)} %reshape.127.pos_col, s32[1,384]{1,0:T(1,128)} %reshape.125.pos_row, f32[1,5120]{1,0:T(1,128)} %gain.1, ...), custom_call_target="tpu_custom_call" | custom-call | tf_op jit(solution)/shard_map/layers/pallas_call | solution.py:470
  166.3 2.9 %copy.15 = bf16[1,1,8,24,5120]{4,3,2,1,0:T(8,128)(2,1)} copy(bf16[1,1,8,24,5120]{4,3,2,1,0:T(8,128)(2,1)} %bitcast.11) | data formatting | bytes 3932160
  (2 shorter events, 0.0 us)

commit v3 on v2

v3 whole, which is shorter than its diff:
```python
import functools

import jax
import jax.numpy as jnp
from jax import lax
from jax.experimental import pallas as pl
from jax.experimental.pallas import tpu as pltpu
from jax.sharding import PartitionSpec as P

HEAD = 128
MESH = pl.DeviceIdType.MESH
RING = 4
PARTS = 8
ORDER = (0, 1, 3, 2)

START, SPREAD, CROSS, RELAY, LAST, UNIT = range(6)
SIGNAL, AWAIT = 12, 13
PROGRAMS = (
    (
        (0, 0, 0), (0, 0, 1), (1, 0, 0, 3), (1, 0, 1, 1), (1, 0, 1, 3), (1, 0, 0, 1), (2, 0, 1, 0),
        (3, 0, 0, 0, 0, 1), (3, 0, 0, 3, 0, 1), (2, 0, 0, 0), (1, 0, 1, 2), (5, 0), (3, 0, 1, 3, 0, 1),
        (3, 0, 0, 0, 0, 3), (3, 0, 1, 1, 0, 1), (3, 0, 1, 3, 0, 3), (1, 0, 0, 2), (2, 0, 0, 1), (3, 0, 0, 3, 0, 3),
        (3, 0, 0, 1, 0, 3), (2, 0, 1, 1), (5, 1), (3, 0, 0, 2, 0, 1), (2, 0, 0, 3), (3, 0, 1, 0, 0, 3),
        (3, 0, 1, 2, 0, 3), (2, 0, 1, 2), (3, 0, 1, 2, 0, 1), (4, 0, 0, 0), (4, 0, 1, 3), (2, 0, 1, 3),
        (3, 0, 0, 1, 0, 1), (2, 0, 0, 2), (3, 0, 1, 0, 0, 1), (4, 0, 0, 3), (3, 0, 1, 1, 1, 3), (3, 0, 0, 1, 1, 3),
        (5, 2), (12, 0), (3, 0, 0, 1, 1, 1), (5, 3), (0, 1, 0), (4, 0, 1, 0), (0, 1, 1), (3, 0, 1, 1, 0, 3),
        (6, 0, 0), (3, 0, 1, 2, 1, 1), (3, 0, 0, 2, 0, 3), (3, 1, 0, 0, 0, 1), (3, 0, 1, 2, 1, 3), (7,),
        (3, 0, 1, 1, 1, 1), (3, 0, 0, 2, 1, 3), (1, 1, 0, 1), (6, 2, 0), (1, 1, 1, 3), (1, 1, 1, 1),
        (3, 0, 0, 2, 1, 1), (6, 0, 1), (6, 1, 0), (1, 1, 0, 3), (2, 1, 1, 0), (6, 2, 1), (3, 1, 1, 0, 0, 3),
        (2, 1, 0, 0), (6, 1, 1), (3, 1, 0, 1, 0, 1), (6, 3, 0), (3, 1, 1, 3, 0, 3), (1, 1, 1, 2), (6, 3, 1),
        (3, 1, 0, 0, 0, 3), (3, 1, 0, 3, 0, 1), (2, 1, 1, 3), (3, 1, 0, 3, 0, 3), (8,), (3, 1, 0, 1, 0, 3),
        (2, 1, 1, 1), (9, 0), (9, 1), (3, 1, 0, 0, 1, 1), (3, 1, 0, 0, 1, 3), (1, 1, 0, 2), (2, 1, 0, 1), (9, 2),
        (9, 3), (9, 4), (2, 1, 1, 2), (10, 0), (4, 1, 0, 1), (2, 1, 0, 2), (3, 1, 1, 2, 0, 3), (3, 1, 1, 1, 0, 1),
        (3, 1, 1, 3, 0, 1), (10, 1), (3, 1, 1, 2, 0, 1), (3, 1, 0, 2, 0, 1), (12, 1), (4, 1, 0, 3), (4, 1, 1, 3),
        (3, 1, 0, 2, 1, 1), (3, 1, 1, 1, 1, 3), (3, 1, 1, 1, 0, 3), (3, 1, 0, 2, 0, 3), (11, 0), (3, 1, 1, 0, 0, 1),
        (3, 1, 1, 1, 1, 1), (3, 1, 0, 2, 1, 3), (2, 1, 0, 3), (3, 1, 1, 2, 1, 3), (3, 1, 1, 2, 1, 1), (11, 1),
        (10, 2), (10, 3), (4, 1, 1, 0), (10, 4), (10, 5), (10, 6), (10, 7), (11, 3), (11, 2), (11, 4), (11, 5),
        (11, 6), (11, 7),
    ),
    (
        (0, 0, 1), (0, 0, 0), (1, 0, 0, 3), (1, 0, 1, 1), (1, 0, 0, 1), (3, 0, 0, 0, 0, 1), (1, 0, 1, 3),
        (3, 0, 1, 0, 0, 3), (0, 1, 1), (1, 0, 0, 2), (5, 0), (3, 0, 1, 3, 0, 1), (3, 0, 0, 0, 0, 3), (2, 0, 1, 1),
        (2, 0, 0, 1), (3, 0, 0, 3, 0, 3), (0, 1, 0), (3, 0, 0, 2, 0, 1), (1, 0, 1, 2), (4, 0, 0, 0),
        (3, 0, 0, 3, 0, 1), (2, 0, 0, 0), (3, 0, 1, 0, 0, 1), (2, 0, 0, 2), (2, 0, 1, 0), (3, 0, 1, 3, 0, 3),
        (3, 1, 0, 0, 0, 1), (1, 1, 0, 1), (4, 0, 0, 3), (2, 1, 0, 0), (2, 0, 0, 3), (3, 0, 1, 1, 1, 1),
        (3, 0, 1, 1, 0, 1), (1, 1, 1, 3), (2, 0, 1, 2), (2, 0, 1, 3), (3, 0, 1, 2, 0, 1), (3, 0, 1, 1, 0, 3), (5, 1),
        (3, 0, 0, 1, 0, 3), (3, 0, 0, 2, 0, 3), (3, 0, 0, 1, 0, 1), (6, 0, 0), (3, 0, 0, 1, 1, 3),
        (3, 0, 0, 1, 1, 1), (3, 0, 0, 2, 1, 1), (4, 0, 1, 3), (6, 0, 1), (3, 0, 0, 2, 1, 3), (4, 0, 1, 0),
        (1, 1, 0, 3), (3, 1, 0, 0, 1, 3), (3, 1, 1, 3, 0, 1), (3, 0, 1, 2, 0, 3), (3, 0, 1, 2, 1, 3), (1, 1, 1, 1),
        (3, 0, 1, 1, 1, 3), (5, 2), (3, 1, 1, 0, 0, 1), (3, 1, 1, 3, 0, 3), (6, 2, 0), (3, 0, 1, 2, 1, 1),
        (3, 1, 0, 1, 0, 1), (2, 1, 1, 3), (3, 1, 0, 0, 0, 3), (3, 1, 0, 0, 1, 1), (5, 3), (7,), (3, 1, 1, 0, 0, 3),
        (2, 1, 0, 1), (6, 2, 1), (6, 1, 0), (2, 1, 1, 0), (3, 1, 0, 1, 0, 3), (6, 3, 0), (6, 1, 1), (1, 1, 1, 2),
        (6, 3, 1), (8,), (2, 1, 1, 1), (1, 1, 0, 2), (9, 0), (9, 1), (2, 1, 1, 2), (9, 2), (9, 3), (9, 4), (10, 0),
        (3, 1, 1, 1, 0, 1), (3, 1, 0, 3, 0, 3), (3, 1, 1, 1, 1, 3), (3, 1, 1, 1, 1, 1), (3, 1, 0, 2, 0, 1),
        (3, 1, 1, 1, 0, 3), (3, 1, 0, 3, 0, 1), (3, 1, 1, 2, 0, 1), (4, 1, 0, 1), (2, 1, 0, 3), (3, 1, 0, 2, 0, 3),
        (2, 1, 0, 2), (3, 1, 1, 2, 0, 3), (3, 1, 1, 2, 1, 1), (10, 1), (4, 1, 0, 3), (4, 1, 1, 3), (4, 1, 1, 0),
        (10, 2), (3, 1, 1, 2, 1, 3), (10, 3), (11, 1), (3, 1, 0, 2, 1, 3), (10, 4), (11, 0), (10, 5),
        (3, 1, 0, 2, 1, 1), (11, 2), (10, 6), (10, 7), (11, 4), (11, 5), (11, 6), (11, 3), (11, 7),
    ),
)


def needs_and_sends(event):
    kind, w, cls = event[:3]
    if kind == START:
        own = (w, cls, 0, 0, 0, None)
        return [], [(own, 0, 1), (own, 0, -1), (own, 2, 0), (own, 1, 1), (own, 1, -1)]
    fo = event[3]
    if kind == SPREAD:
        whole = (w, cls, 0, fo, 0, None)
        needs = [whole] if fo != 2 else [whole[:5] + (0,), whole[:5] + (1,)]
        sends = []
        if fo == 3:
            sends.append((whole[:5] + (0,), 0, 1))
        if fo == 1:
            sends.append((whole[:5] + (1,), 0, -1))
        return needs, sends + [(whole, 2, 0), (whole, 1, 1), (whole, 1, -1)]
    if kind == CROSS:
        whole = (w, cls, 1, fo, 0, None)
        return [whole], [(whole, 1, 1), (whole, 1, -1)]
    if kind == RELAY:
        who, go = event[4:]
        whole = (w, cls, who, fo, go, None)
        return [whole], [(whole[:5] + (0 if go == 3 else 1,), 1, 1 if go == 3 else -1)]
    whole = (w, cls, 0, fo, 2, None)
    return [whole[:5] + (0,), whole[:5] + (1,)], [(whole, 2, 0)]


def landing(piece, link, step):
    w, cls, who, fo, go, h = piece
    if link == 0:
        return (w, cls, who, (fo - step) % RING, go, h)
    if link == 1:
        return (w, cls, who, fo, (go - step) % RING, h)
    return (w, cls, 1 - who, fo, go, h)


def in_slab(piece, offset):
    return (piece[3] if piece[1] == 0 else piece[4]) == offset


def layer_kernel(
    quarter, tok, docs, gain, wq, wot, wk, wv, out,
    full_q, full_o, kv_w, hidden, scaled, level, acc_q, acc_kv, query, kv_made, kv, attended, bias, part, part_in,
    w_recv, w_send, own_sem, swap_send, kvw_sem, kv_sem, kv_send, h_sem, h_send, p_recv, p_send, n_send, gate,
):
    section = lax.axis_index("section")
    dp = lax.axis_index("dp")
    tensor = lax.axis_index("tensor")
    z, y, far = dp // 8, (dp // 2) % RING, dp % 2
    rows, width = tok.shape
    seq = 2 * rows
    block, q_width = wq.shape
    half = block // 2
    small = half // 32 * 16
    chunk = width // PARTS
    slab = 2 * chunk
    kv_width = wk.shape[1]
    weights = (full_q, full_o)
    shards = (wq, wot)

    z_of = [lax.rem(z + d, RING) * 8 for d in range(RING)]
    y_of = [lax.rem(y + d, RING) * 2 for d in range(RING)]
    whose_of = [far, 1 - far]
    z_row, y_row, x_row = ([dp_part * block for dp_part in parts] for parts in (z_of, y_of, whose_of))

    def at(dz, dy):
        return (section, z_of[dz % RING] + y_of[dy % RING] + far, tensor)

    opposite = (section, z_of[0] + y_of[0] + (1 - far), 1 - tensor)
    partner = (section, dp, 1 - tensor)
    core = (1 - section, dp, tensor)
    partner_core = (1 - section, dp, 1 - tensor)
    peers = [at(1, 0), at(-1, 0), at(0, 1), at(0, -1), opposite, partner, core, partner_core]
    barrier = pltpu.get_barrier_semaphore()
    for peer in peers:
        pl.semaphore_signal(barrier, inc=1, device_id=peer, device_id_type=MESH)

    def place(piece):
        w, cls, who, fo, go, h = piece
        dz, dy = (fo, go) if cls == 0 else (go, fo)
        first = z_row[dz] + y_row[dy] + x_row[who] + cls * half
        large = half - small
        cut = large if who == 0 else small
        size = half
        if h == 0:
            size = cut
        if h == 1:
            first, size = first + cut, half - cut
        return weights[w].at[pl.ds(pl.multiple_of(first, 16), size), :]

    def number(piece):
        w, cls, who, fo, go, h = piece
        return w, cls, who, fo * RING + go, 1 if h == 1 else 0

    def copy_of(piece, link, step):
        name = landing(piece, link, step)
        if link == 2:
            target = opposite
        else:
            target = at(step, 0) if link == piece[1] else at(0, step)
        return pltpu.make_async_remote_copy(
            src_ref=place(piece), dst_ref=place(piece), send_sem=w_send.at[number(name)],
            recv_sem=w_recv.at[number(name)], device_id=target, device_id_type=MESH,
        )

    def await_piece(piece):
        ref = place(piece)
        pltpu.make_async_copy(ref, ref, w_recv.at[number(piece)]).wait()

    def own_copy(w, cls):
        return pltpu.make_async_copy(
            shards[w].at[pl.ds(cls * half, half), :], place((w, cls, 0, 0, 0, None)), own_sem.at[w, cls]
        )

    def swap_copy(w, cls):
        return pltpu.make_async_remote_copy(
            src_ref=shards[w].at[pl.ds(cls * half, half), :], dst_ref=place((w, cls, 0, 0, 0, None)),
            send_sem=swap_send.at[w, cls], recv_sem=own_sem.at[w, cls], device_id=partner, device_id_type=MESH,
        )

    def signal_core():
        @pl.when(section == 0)
        def _():
            pl.semaphore_signal(gate, inc=1, device_id=core, device_id_type=MESH)

    def run(event):
        needs, sends = needs_and_sends(event)
        if event[0] == START:
            own_copy(*event[1:]).wait()
        for piece in needs:
            await_piece(piece)
        for send in sends:
            copy_of(*send).start()

    events = [step for step in PROGRAMS[0] if step[0] < UNIT]
    all_sends = [send for event in events for send in needs_and_sends(event)[1]]
    awaited = {piece for event in events for piece in needs_and_sends(event)[0]}

    def rest_of(w, offset):
        for send in all_sends:
            name = landing(*send)
            if name[0] == w and name not in awaited and in_slab(name, offset):
                await_piece(name)

    def rows_of(which):
        return pl.ds(pl.multiple_of(which * rows, 16), rows)

    def cols_of(k):
        first = ((z + ORDER[k // 2]) % RING) * slab + (k % 2) * chunk
        return pl.ds(pl.multiple_of(first, 128), chunk)

    def slab_of(j):
        return pl.ds(pl.multiple_of(((z + ORDER[j]) % RING) * slab, 128), slab)

    kvw_copies = [
        pltpu.make_async_copy(wk, kv_w.at[0], kvw_sem.at[0]),
        pltpu.make_async_copy(wv, kv_w.at[1], kvw_sem.at[1]),
    ]

    def token_copy(k):
        return pltpu.make_async_copy(
            tok.at[:, cols_of(k)], hidden.at[rows_of(tensor), cols_of(k)], h_sem.at[0, k]
        )

    def token_send(k):
        return pltpu.make_async_remote_copy(
            src_ref=tok.at[:, cols_of(k)], dst_ref=hidden.at[rows_of(tensor), cols_of(k)],
            send_sem=h_send.at[k], recv_sem=h_sem.at[1, k], device_id=partner, device_id_type=MESH,
        )

    def swap(w):
        @pl.when(far == 1)
        def _():
            for cls in (0, 1):
                swap_copy(w, cls).start()

    @pl.when(far == 0)
    def _():
        for w in (0, 1):
            for cls in (0, 1):
                own_copy(w, cls).start()

    pl.semaphore_wait(barrier, len(peers))

    @pl.when(section == 0)
    def _():
        swap(0)
        for k in range(PARTS):
            token_copy(k).start()
            token_send(k).start()
        swap(1)

    for copy in kvw_copies:
        copy.start()

    def settle():
        for copy in kvw_copies:
            copy.wait()

        def position(index):
            upper = jnp.where(index >= rows, 1, 0)
            segment = sum(jnp.where(index - rows * upper >= quarter * n, 1, 0) for n in range(1, rows // quarter))
            return index - upper * (rows - quarter) + segment * quarter

        here = position(lax.broadcasted_iota(jnp.int32, (seq, seq), 1))
        pick = jnp.where(lax.broadcasted_iota(jnp.int32, (seq, seq), 0) == here, 1.0, 0.0)
        along = jnp.broadcast_to(docs[...].astype(jnp.float32), (8, seq))
        docs_row = jnp.dot(along, pick, preferred_element_type=jnp.float32)[:1, :]
        there = position(lax.broadcasted_iota(jnp.int32, (seq, seq), 0))
        pick = lax.broadcasted_iota(jnp.int32, (seq, seq), 1) == there
        docs_col = jnp.sum(jnp.where(pick, docs[...].astype(jnp.float32), 0.0), axis=-1, keepdims=True)
        bias[...] = jnp.where((here <= there) & (docs_row == docs_col), 0.0, -1e30)

    step_rows = 32

    def prepare(j):
        for k in (2 * j, 2 * j + 1):
            for src, whose in ((0, tensor), (1, 1 - tensor)):
                ref = hidden.at[rows_of(whose), cols_of(k)]
                pltpu.make_async_copy(ref, ref, h_sem.at[src, k]).wait()
        cols = slab_of(j)

        def body(i, carry):
            here = pl.ds(pl.multiple_of(i * step_rows, step_rows), step_rows)
            wide = hidden[here, cols].astype(jnp.float32)
            scaled[j, here, :] = (wide * gain[:, cols]).astype(jnp.bfloat16)
            total = jnp.sum(wide * wide, axis=-1, keepdims=True)
            level[here, :] = total if j == 0 else level[here, :] + total
            return carry

        lax.fori_loop(0, seq // step_rows, body, 0)
        for i in (0, 1):
            cols_i = pl.ds(i * kv_width, kv_width)
            term = jnp.dot(scaled[j], kv_w[i, slab_of(j), :], preferred_element_type=jnp.float32)
            acc_kv[:, cols_i] = term if j == 0 else acc_kv[:, cols_i] + term

    tile = 256

    def project(j, part):
        if part == 0:
            rest_of(0, ORDER[j])

        def body(i, carry):
            cols = pl.ds(pl.multiple_of(i * tile, tile), tile)
            term = jnp.dot(scaled[j], full_q[slab_of(j), cols], preferred_element_type=jnp.float32)
            acc_q[:, cols] = term if j == 0 else acc_q[:, cols] + term
            return carry

        lax.fori_loop((0, 3)[part], (3, q_width // tile)[part], body, 0)

    def kv_exchange(i):
        return pltpu.make_async_remote_copy(
            src_ref=kv_made.at[i], dst_ref=kv.at[i], send_sem=kv_send.at[i], recv_sem=kv_sem.at[i],
            device_id=partner, device_id_type=MESH,
        )

    def kv_keep(i):
        return pltpu.make_async_copy(kv_made.at[i], kv.at[i], kv_sem.at[i])

    def finish_kv():
        factor = lax.rsqrt(level[...] / width + 1e-06)
        level[...] = factor
        for i in (0, 1):
            kv_made[i] = (acc_kv[:, i * kv_width : (i + 1) * kv_width] * factor).astype(jnp.bfloat16)

            @pl.when(far == 1)
            def _():
                kv_exchange(i).start()

            @pl.when(far == 0)
            def _():
                kv_keep(i).start()

    def finish_q():
        for i in range(q_width // tile):
            query[:, i * tile : (i + 1) * tile] = (acc_q[:, i * tile : (i + 1) * tile] * level[...]).astype(jnp.bfloat16)

    scale = 1.0 / HEAD**0.5
    heads = q_width // HEAD
    group = heads // (kv_width // HEAD)

    def attend(pair):
        if pair == 0:
            for i in (0, 1):
                kv_keep(i).wait()
        for h in (2 * pair, 2 * pair + 1):
            cols = slice(h * HEAD, (h + 1) * HEAD)
            kv_cols = slice(h // group * HEAD, (h // group + 1) * HEAD)
            scores = lax.dot_general(
                query[:, cols], kv[0, :, kv_cols], (((1,), (1,)), ((), ())), preferred_element_type=jnp.float32
            )
            scores = scores * scale + bias[...]
            scores = jnp.exp(scores - jnp.max(scores, axis=-1, keepdims=True))
            mix = (scores / jnp.sum(scores, axis=-1, keepdims=True)).astype(jnp.bfloat16)
            attended[:, cols] = jnp.dot(
                mix, kv[1, :, kv_cols], preferred_element_type=jnp.float32
            ).astype(jnp.bfloat16)

    def part_send(k):
        return pltpu.make_async_remote_copy(
            src_ref=part.at[k, rows_of(1 - tensor), :], dst_ref=part_in.at[k],
            send_sem=p_send.at[k], recv_sem=p_recv.at[k], device_id=partner, device_id_type=MESH,
        )

    def next_send(k, side):
        return pltpu.make_async_remote_copy(
            src_ref=out.at[:, cols_of(k)], dst_ref=hidden.at[rows_of(tensor), cols_of(k)],
            send_sem=n_send.at[side, k], recv_sem=h_sem.at[side, k],
            device_id=core if side == 0 else partner_core, device_id_type=MESH,
        )

    def finish(k):
        part_send(k).wait_recv()
        own = hidden[rows_of(tensor), cols_of(k)].astype(jnp.float32)
        update = part[k, rows_of(tensor), :].astype(jnp.float32) + part_in[k].astype(jnp.float32)
        out[:, cols_of(k)] = (own + update).astype(jnp.bfloat16)

        @pl.when(section == 0)
        def _():
            next_send(k, 0).start()
            next_send(k, 1).start()

    def multiply(k):
        if k % 2 == 0:
            rest_of(1, ORDER[k // 2])
        result = lax.dot_general(
            attended[...], full_o[cols_of(k), :], (((1,), (1,)), ((), ())), preferred_element_type=jnp.float32
        )
        part[k] = result.astype(jnp.bfloat16)
        part_send(k).start()

    units = (prepare, project, finish_kv, finish_q, attend, multiply, finish)

    def program(steps, settled):
        for step in steps:
            if step[0] < UNIT:
                run(step)
                continue
            if step[0] == SIGNAL:
                signal_core()
            elif step[0] == AWAIT:
                pl.semaphore_wait(gate, 1)
            else:
                if step == (UNIT, 0) and not settled:
                    settle()
                units[step[0] - UNIT](*step[1:])

    @pl.when(section == 0)
    def _():
        program(PROGRAMS[0], False)

    @pl.when(section == 1)
    def _():
        settle()
        pl.semaphore_wait(gate, 1)
        for w in (0, 1):
            swap(w)
        pl.semaphore_wait(gate, 1)
        program(PROGRAMS[1], True)

    for send in all_sends:
        copy_of(*send).wait_send()
    for k in range(PARTS):
        part_send(k).wait_send()

    @pl.when(far == 1)
    def _():
        for w in (0, 1):
            for cls in (0, 1):
                swap_copy(w, cls).wait_send()
        for i in (0, 1):
            kv_exchange(i).wait_send()

    @pl.when(section == 0)
    def _():
        for k in range(PARTS):
            token_send(k).wait_send()
            next_send(k, 0).wait_send()
            next_send(k, 1).wait_send()


def on_device(tokens, doc_ids, norm_gain, w_query, w_key, w_value, w_out):
    n_segments, quarter, width = tokens.shape[1:]
    rows = n_segments * quarter
    seq = 2 * rows
    block, q_width = w_query.shape[1:]
    kv_width = w_key.shape[2]
    chunk = width // PARTS
    bf16, f32 = jnp.bfloat16, jnp.float32
    dma = pltpu.SemaphoreType.DMA
    anywhere = pl.BlockSpec(memory_space=pl.ANY)
    vmem = pl.BlockSpec(memory_space=pltpu.VMEM)
    state = pl.pallas_call(
        functools.partial(layer_kernel, quarter),
        out_shape=pltpu.VMEM((rows, width), bf16),
        in_specs=[anywhere, vmem, vmem] + [anywhere] * 4,
        out_specs=vmem,
        scratch_shapes=[
            pltpu.VMEM((width, q_width), bf16),
            pltpu.VMEM((width, q_width), bf16),
            pltpu.VMEM((2, width, kv_width), bf16),
            pltpu.VMEM((seq, width), bf16),
            pltpu.VMEM((RING, seq, 2 * chunk), bf16),
            pltpu.VMEM((seq, 1), f32),
            pltpu.VMEM((seq, q_width), f32),
            pltpu.VMEM((seq, 2 * kv_width), f32),
            pltpu.VMEM((seq, q_width), bf16),
            pltpu.VMEM((2, seq, kv_width), bf16),
            pltpu.VMEM((2, seq, kv_width), bf16),
            pltpu.VMEM((seq, q_width), bf16),
            pltpu.VMEM((seq, seq), f32),
            pltpu.VMEM((PARTS, seq, chunk), bf16),
            pltpu.VMEM((PARTS, rows, chunk), bf16),
            dma((2, 2, 2, RING * RING, 2)),
            dma((2, 2, 2, RING * RING, 2)),
            dma((2, 2)),
            dma((2, 2)),
            dma((2,)),
            dma((2,)),
            dma((2,)),
            dma((2, PARTS)),
            dma((PARTS,)),
            dma((PARTS,)),
            dma((PARTS,)),
            dma((2, PARTS)),
            pltpu.SemaphoreType.REGULAR,
        ],
        compiler_params=pltpu.CompilerParams(
            collective_id=0, has_side_effects=True, vmem_limit_bytes=60 * 1024 * 1024
        ),
        name="layers",
    )(
        tokens[0].reshape(rows, width),
        doc_ids,
        norm_gain,
        w_query[0],
        w_out[0].T,
        w_key[0],
        w_value[0],
    )
    return state.reshape(1, 1, n_segments, quarter, width)


def solution(mesh):
    in_specs = (
        P("dp", None, "tensor", None),
        P("dp", None),
        P("section", None),
        P("section", "dp", "tensor"),
        P("section", None, "tensor"),
        P("section", None, "tensor"),
        P("section", "tensor", "dp"),
    )
    out_specs = P("section", "dp", None, "tensor", None)
    return jax.shard_map(
        on_device, mesh=mesh, in_specs=in_specs, out_specs=out_specs, check_vma=False
    )
```

time: 169 us -> 156 us (0.923)
  Pallas kernels: 163 us -> 155 us
  local copies, waits for them, and re-layouts: 5.94 us -> 1.27 us
    pallas_call x1, Pallas kernels: 163 us -> 155 us  [on_device(): pl.pallas_call(functools.partial(layer_kernel, quarter), out_shape=pltpu....]
where the time goes in v3:
time: 156 us
  Pallas kernels  155 us (99%)
    pallas_call x1, Pallas kernels, on_device(): pl.pallas_call(functools.partial(layer_kernel, quarter), out_shape=pltpu....  155 us

profile of v3, /device:TPU:1, one launch (start us, length us, event | category | flops | bytes accessed | tf_op | source)
XLA Modules:
  0.0 156.2 jit_solution(14664441554474168193)
XLA Ops:
  0.0 154.9 %layers.1 = bf16[192,5120]{1,0:T(8,128)(2,1)S(1)} custom-call(bf16[192,5120]{1,0:T(8,128)(2,1)} %bitcast.11, s32[1,384]{1,0:T(1,128)} %docs.1, f32[1,5120]{1,0:T(1,128)} %gain.1, bf16[160,1280]{1,0:T(8,128)(2,1)} %bitcast.12, bf16[160,1280]{1,0:T(8,128)(2,1)} %bitcast.13, bf16[5120,256]{1,0:T(8,128)(2,1)} %bitcast.9, bf16[5120,256]{1,0:T(8,128)(2,1)} %bitcast.10), custom_call_target="tpu_custom_call" | custom-call | tf_op jit(solution)/shard_map/layers/pallas_call | solution.py:454
  154.9 1.3 copy.9
